TPU v7x, 512 devices: a whole 4x8x8 slice. The times are simulated.
512 devices in a mesh: slab: 64 (over y_lo, z, core), head: 8 (over x, y_hi).
Axes of the slice: x: 4, y: 8 (y_hi: 2, y_lo: 4; y = y_hi * 4 + y_lo), z: 8, core: 2. Of those that a mesh axis runs over, the one named last changes fastest.
Arguments:
- query: bfloat16 [16384, 2048], P(('slab', 'head')), may hold values from -12 to 12
- key: bfloat16 [16384, 2048], P(('slab', 'head')), may hold values from -4 to 4
- value: bfloat16 [16384, 2048], P(('slab', 'head')), may hold values from -6 to 6
- grad_out: bfloat16 [16384, 2048], P(('slab', 'head')), may hold values from -6 to 6
- query_scale: float32 [2048], replicated, may hold values from 0.5 to 2
- key_scale: float32 [2048], replicated, may hold values from 0.5 to 2
- neighbours: int32 [256, 27], P('slab'), may hold values from 0 to 255, as said below
Outputs:
- attention: bfloat16 [16384, 2048], P(('slab', 'head'))
- grad_query: bfloat16 [16384, 2048], P(('slab', 'head'))
- grad_key: bfloat16 [16384, 2048], P(('slab', 'head'))
- grad_value: bfloat16 [16384, 2048], P(('slab', 'head'))
Inputs may be any that keep to these rules, and one draw needn't show every extreme that they name: `neighbours`: row t lists tiles of the 3 x 3 x 3 window of tiles around tile t (frame tile, row and column offsets -1, 0, 1 in slot order frame-major), clipped at the grid's edges, with some window tiles left out; tile t itself is always listed, and every unused slot repeats t.
All inputs are finite; a program needn't handle non-finite values.
Results may differ from a plain program's by a relative error of at most 0.039.
Values may be sent and summed in bfloat16 or wider, within the bound.
A program may use at most 64 MiB of HBM per device.

v0:
```python
import functools

import jax
import jax.numpy as jnp
from jax import lax
from jax.experimental import pallas as pl
from jax.experimental.pallas import tpu as pltpu
from jax.sharding import PartitionSpec as P

HD = 128
TILE = 64
FT = 4
TW = 4
SLAB = TILE * TW
RING = 2 * FT
BLOCKS = 9
OUTER, INNER, BEYOND = 0, 1, 2
HIDDEN = -1e30
MESH = pl.DeviceIdType.MESH
BF16 = jnp.bfloat16
F32 = jnp.float32
KEY, VALUE, QUERY, GRAD = range(4)
KV, QD = range(2)
ARRAYS = (pl.ds(0, 2), pl.ds(2, 2))
VMEM_BYTES = 58 * 1024 * 1024


def dot_nn(a, b):
    return lax.dot_general(a, b, (((1,), (0,)), ((), ())), preferred_element_type=F32)


def dot_nt(a, b):
    return lax.dot_general(a, b, (((1,), (1,)), ((), ())), preferred_element_type=F32)


def dot_tn(a, b):
    return lax.dot_general(a, b, (((0,), (0,)), ((), ())), preferred_element_type=F32)


def add_rows(scores, rows):
    shaped = scores.reshape(3, TILE, scores.shape[1]) + rows[:, None, :]
    return shaped.reshape(scores.shape)


def join(low, high, both):
    return jnp.concatenate(
        [low[:TILE], both(low[TILE:], high[: 2 * TILE]), high[2 * TILE :]], axis=0
    )


def fold(array, both):
    return both(both(array[:, :128], array[:, 128:256]), array[:, 256:])


def wide(column):
    return jnp.concatenate([column] * 3, axis=1)


def near(half):
    return slice(half * TILE, half * TILE + 3 * TILE)


def own(half):
    return slice(half * 2 * TILE, (half + 1) * 2 * TILE)


def kernel(
    rows, columns,
    query, key, value, grad_out, query_scale_in, key_scale_in, neighbours_in, landed,
    raw, query_scale, key_scale, neighbours,
    stage, data, listed, lists, bias, bias_rows, scores, weights, inverses, log_totals, kept, key_sums,
    stats, stats_sent, results,
    in_sem, a2a_send, a2a_recv, list_send, list_recv, halo_send, y_recv, r_recv,
    stat_send, stat_recv, far_send, far_recv, out_send, out_recv,
):
    loads = [
        pltpu.make_async_copy(source, target, in_sem.at[i])
        for i, (source, target) in enumerate((
            (key, raw.at[0]), (value, raw.at[1]), (query, raw.at[2]), (grad_out, raw.at[3]),
            (key_scale_in, key_scale), (query_scale_in, query_scale),
            (neighbours_in, neighbours),
        ))
    ]
    for load in (loads[4], *loads[:4], *loads[5:]):
        load.start()

    slab = lax.axis_index("slab")
    head = lax.axis_index("head")
    y_lo, r = slab // rows, slab % rows
    x, y_hi = head // 2, head % 2
    y = y_hi * FT + y_lo
    chunk = SLAB // (2 * columns)
    half = 1 - y_lo // 2
    far_y = (1 - y_lo // 2) * 2
    y_far = (far_y, far_y + 1, far_y + FT, far_y + FT + 1)
    frame_of = (3 * half, 1 + half, 2 - half)

    def quarter(at_y):
        return ((at_y + RING - 1) % RING) // 2

    def slot_of(at_y):
        return ((at_y % FT + 1) % FT) // 2

    my_head = x * 4 + quarter(y)
    y_partner = (y + RING - 1 + 2 * (y % 2)) % RING

    def device(to_y, to_r, to_x):
        return {"slab": (to_y % FT) * rows + to_r, "head": to_x * 2 + to_y // FT}

    r_at = ((r + rows - 1) % rows, r, (r + 1) % rows)
    x_at = tuple((x + step) % columns for step in range(columns))

    def at_side(side):
        return pl.when(r < rows - 1) if side == 2 else pl.when(r >= 1 - side)

    barrier = pltpu.get_barrier_semaphore()

    def greet(peers):
        for peer in peers:
            pl.semaphore_signal(barrier, 1, device_id=peer, device_id_type=MESH)

    greet([device(to_y, r, to_x) for to_y in y_far for to_x in x_at])
    greet([device(y_partner, r, x)])
    for side in (0, 2):
        @at_side(side)
        def _():
            greet([device(y, r_at[side], x), device(y_partner, r_at[side], x)])

    listed[...] = jnp.full(listed.shape, -2.0, F32)

    def put(which, array):
        for piece in range(4 * columns):
            stage[which, piece] = array[:, piece * HD : (piece + 1) * HD]

    loads[4].wait()
    loads[0].wait()
    put(KEY, (raw[0].astype(F32) * key_scale[...]).astype(BF16))
    loads[1].wait()
    put(VALUE, raw[1])
    row_sides = (r + rows - 1) // rows + (2 * rows - 2 - r) // rows
    pl.semaphore_wait(barrier, 4 * columns + 1 + 2 * row_sides)

    my_rows = pl.ds(pl.multiple_of(head * chunk, chunk), chunk)

    def send_heads(kind, places):
        for to_x in x_at:
            for to_y in places:
                pltpu.make_async_remote_copy(
                    src_ref=stage.at[ARRAYS[kind], to_x * 4 + quarter(to_y)],
                    dst_ref=data.at[ARRAYS[kind], slot_of(y), 1, my_rows, :],
                    send_sem=a2a_send.at[kind],
                    recv_sem=a2a_recv.at[kind, slot_of(y)],
                    device_id=device(to_y, r, to_x),
                    device_id_type=MESH,
                ).start()

    def wait_heads(kind, slot):
        whole = data.at[ARRAYS[kind], slot, 1]
        pltpu.make_async_copy(whole, whole, a2a_recv.at[kind, slot]).wait()

    def y_copy(kind):
        return pltpu.make_async_remote_copy(
            src_ref=data.at[ARRAYS[kind], INNER, 1],
            dst_ref=data.at[ARRAYS[kind], BEYOND, 1],
            send_sem=halo_send.at[kind, 6],
            recv_sem=y_recv.at[kind],
            device_id=device(y_partner, r, x),
            device_id_type=MESH,
        )

    def start_rows(copies):
        for side, copy in copies.items():
            at_side(side)(copy.start)

    def sent_rows(copies):
        for side, copy in copies.items():
            at_side(side)(copy.wait_send)

    def came_rows(copies):
        for side, copy in copies.items():
            at_side(2 - side)(copy.wait_recv)

    def r_copies(kind, slot):
        return {
            side: pltpu.make_async_remote_copy(
                src_ref=data.at[ARRAYS[kind], slot, 1],
                dst_ref=data.at[ARRAYS[kind], slot, 2 - side],
                send_sem=halo_send.at[kind, slot * 2 + side // 2],
                recv_sem=r_recv.at[kind, slot, side // 2],
                device_id=device(y, r_at[side], x),
                device_id_type=MESH,
            )
            for side in (0, 2)
        }

    def spread(kind, slot):
        start_rows(r_copies(kind, slot))

    def forward(kind):
        y_copy(kind).wait_recv()
        spread(kind, BEYOND)

    def wait_rows(kind, slot):
        came_rows(r_copies(kind, slot))

    send_heads(KV, y_far)
    loads[6].wait()
    listed[0:TW, 0:27] = neighbours[...].astype(F32)
    for to_y in y_far:
        pltpu.make_async_remote_copy(
            src_ref=listed, dst_ref=lists.at[y_hi, slot_of(y)],
            send_sem=list_send, recv_sem=list_recv,
            device_id=device(to_y, r, x), device_id_type=MESH,
        ).start()

    loads[5].wait()
    factor = query_scale[...] * HD ** (-0.5)
    loads[2].wait()
    put(QUERY, (raw[2].astype(F32) * factor).astype(BF16))
    loads[3].wait()
    put(GRAD, raw[3])
    send_heads(QD, y_far)

    for side in (0, 2):
        @pl.when(r == (rows - 1 if side == 2 else 0))
        def _():
            data[:, :, side] = jnp.zeros((4, 3, SLAB, HD), BF16)
            stats[:, side] = jnp.full((3, 2, 8, SLAB), HIDDEN, F32)

    wait_heads(KV, INNER)
    y_copy(KV).start()
    spread(KV, INNER)
    wait_heads(KV, OUTER)
    spread(KV, OUTER)

    pltpu.make_async_copy(lists, lists, list_recv).wait()
    shape = (BLOCKS * 8, 128)
    line = lax.broadcasted_iota(jnp.int32, shape, 0)
    column = line % 8
    block_of = line // 8
    key_slot = block_of // 3
    key_frame = jnp.where(
        key_slot == 0, frame_of[0], jnp.where(key_slot == 1, frame_of[1], frame_of[2])
    )
    key_row = r + block_of % 3 - 1
    real = (column < TW) & (key_row >= 0) & (key_row < rows)
    ids = jnp.where(real, (key_frame * rows + key_row) * TW + column, -5).astype(F32)
    lane_tile = lax.broadcasted_iota(jnp.int32, (BLOCKS * 8, SLAB), 1) // TILE
    lane = lax.broadcasted_iota(jnp.int32, (8, 128), 1)
    for slot in (OUTER, INNER):
        found = jnp.full((BLOCKS * 8, SLAB), HIDDEN, F32)
        for tile in range(TW):
            hit = jnp.max(
                jnp.where(lists[0, slot, tile : tile + 1, :] == ids, 0.0, HIDDEN),
                axis=1, keepdims=True,
            )
            found = jnp.where(lane_tile == tile, hit, found)
        bias[slot] = found.reshape(BLOCKS, 8, SLAB)
        turned = jnp.concatenate(
            [
                jnp.concatenate(
                    [found[:, tile * TILE : tile * TILE + 1] for tile in range(TW)]
                    + [jnp.full((BLOCKS * 8, 124), HIDDEN, F32)],
                    axis=1,
                ),
                jnp.full((56, 128), HIDDEN, F32),
            ],
            axis=0,
        ).T[:8]
        for key_block in range(BLOCKS):
            for side in range(2):
                at = key_block * 8 + side * 2
                bias_rows[slot, key_block // 3, side, :, pl.ds(key_block % 3 * 128, 128)] = jnp.where(
                    lane < TILE, turned[:, at : at + 1], turned[:, at + 1 : at + 2]
                )

    wait_heads(QD, INNER)
    y_copy(QD).start()
    wait_heads(QD, OUTER)
    spread(QD, OUTER)

    def return_heads(kind, slot):
        for to_x in x_at:
            for far_hi in range(2):
                to_y = frame_of[slot] + far_hi * FT
                token_chunk = to_x * 2 + far_hi
                part = pl.ds(pl.multiple_of(token_chunk * chunk, chunk), chunk)
                pltpu.make_async_remote_copy(
                    src_ref=results.at[kind, slot, :, part, :],
                    dst_ref=landed.at[kind, my_head],
                    send_sem=out_send.at[kind],
                    recv_sem=out_recv.at[kind],
                    device_id=device(to_y, r, to_x),
                    device_id_type=MESH,
                ).start()

    def my_scale(scale):
        return scale[:, pl.ds(pl.multiple_of(my_head * HD, HD), HD)]

    def stat_copies(slot):
        return {
            side: pltpu.make_async_remote_copy(
                src_ref=stats_sent.at[slot, side, 0:2],
                dst_ref=stats.at[slot, 2 - side],
                send_sem=stat_send.at[slot, side // 2],
                recv_sem=stat_recv.at[slot, side // 2],
                device_id=device(y, r_at[side], x),
                device_id_type=MESH,
            )
            for side in (0, 2)
        }

    def far_stat_copies():
        return {
            side: pltpu.make_async_remote_copy(
                src_ref=stats_sent.at[INNER, side, BEYOND],
                dst_ref=stats.at[BEYOND, 2 - side, INNER],
                send_sem=far_send.at[side],
                recv_sem=far_recv.at[side],
                device_id=device(y_partner, r_at[side], x),
                device_id_type=MESH,
            )
            for side in range(3)
        }

    def rows_of(array, slot, side):
        return jnp.concatenate(
            [data[array, slot, row, own(side), :] for row in range(3)], axis=0
        )

    def attend(slot, key_slots, arrive, least, between):
        parts = [(key_slot, side) for key_slot in key_slots for side in range(2)]
        peak = [jnp.full((3 * TILE, 128), -3e38, F32) for side in range(2)]
        for key_slot, side in parts:
            if side == 0:
                arrive(key_slot)
            part = add_rows(
                dot_nt(data[QUERY, slot, 1, near(side), :], rows_of(KEY, key_slot, side)),
                bias_rows[slot, key_slot, side, side : side + 3, :],
            )
            scores[key_slot, side] = part
            peak[side] = jnp.maximum(peak[side], fold(part, jnp.maximum))
        row_max = jnp.max(join(*peak, jnp.maximum), axis=1, keepdims=True)
        between()
        row_wide = jnp.maximum(jnp.broadcast_to(row_max, (SLAB, 128)), least)
        totals = [jnp.zeros((3 * TILE, 128), F32) for side in range(2)]
        sums = [jnp.zeros((3 * TILE, HD), F32) for side in range(2)]
        for key_slot, side in parts:
            part = jnp.exp(scores[key_slot, side] - wide(row_wide[near(side)]))
            low = part.astype(BF16)
            weights[slot, key_slot, side] = low
            totals[side] = totals[side] + fold(part, jnp.add)
            sums[side] = sums[side] + dot_nn(low, rows_of(VALUE, key_slot, side))
        total = jnp.sum(join(*totals, jnp.add), axis=1, keepdims=True)
        return row_wide, jnp.broadcast_to(total, (SLAB, 128)), join(*sums, jnp.add)

    def settle(slot, row_wide, total, summed, earlier):
        inverse = 1.0 / total
        results[0, slot, 0] = (summed * inverse).astype(BF16)
        inverses[slot, 0] = inverse * earlier
        inverses[slot, 1] = inverse
        log_totals[slot] = row_wide + jnp.log(total)

    def tell(slot):
        grads = data[GRAD, slot, 1].astype(F32)
        delta = jnp.sum(results[0, slot, 0].astype(F32) * grads, axis=1, keepdims=True)
        lane = lax.broadcasted_iota(jnp.int32, (SLAB, 128), 1)
        turned = jnp.where(lane == 0, log_totals[slot], delta).T
        log_row, delta_row = turned[0:1], turned[1:2]
        line8 = lax.broadcasted_iota(jnp.int32, (8, SLAB), 0)
        for key_slot in (OUTER, INNER) if slot == OUTER else (OUTER, INNER, BEYOND):
            for row in range(3):
                message = jnp.where(
                    line8 == TW, delta_row, bias[slot, key_slot * 3 + row] - log_row
                )
                if row == 1 and key_slot != BEYOND:
                    stats[slot, 1, key_slot] = message
                else:
                    stats_sent[slot, row, key_slot] = message
        start_rows(stat_copies(slot))
        if slot == INNER:
            start_rows(far_stat_copies())
        return delta

    def query_side(slot, delta):
        sums = [jnp.zeros((3 * TILE, HD), F32) for side in range(2)]
        for key_slot in (INNER, OUTER) if slot == OUTER else (INNER, OUTER, BEYOND):
            inverse = inverses[slot, 1 if key_slot == BEYOND else 0]
            delta_part = delta * inverse
            for side in range(2):
                grad_weights = dot_nt(
                    data[GRAD, slot, 1, near(side), :], rows_of(VALUE, key_slot, side)
                )
                part = weights[slot, key_slot, side].astype(F32) * (
                    grad_weights * wide(inverse[near(side)]) - wide(delta_part[near(side)])
                )
                sums[side] = sums[side] + dot_nn(
                    part.astype(BF16), rows_of(KEY, key_slot, side)
                )
        scale = my_scale(query_scale) * HD ** (-0.5)
        results[0, slot, 1] = (join(*sums, jnp.add) * scale).astype(BF16)
        return_heads(0, slot)

    def key_part(slot, query_slot):
        for side in range(2):
            message = jnp.concatenate(
                [stats[query_slot, row, slot, :, own(side)] for row in range(3)], axis=1
            )
            queries = rows_of(QUERY, query_slot, side)
            grads = rows_of(GRAD, query_slot, side)
            part = jnp.exp(add_rows(
                dot_nt(data[KEY, slot, 1, near(side), :], queries), message[side : side + 3]
            ))
            grad_weights = dot_nt(data[VALUE, slot, 1, near(side), :], grads)
            slopes = (part * (grad_weights - message[TW : TW + 1])).astype(BF16)
            for which, term in (
                (0, dot_nn(slopes, queries)), (1, dot_nn(part.astype(BF16), grads))
            ):
                if query_slot == OUTER:
                    key_sums[slot, which, side] = term
                else:
                    key_sums[slot, which, side] += term

    def key_end(slot):
        grad_keys = join(key_sums[slot, 0, 0], key_sums[slot, 0, 1], jnp.add)
        grad_values = join(key_sums[slot, 1, 0], key_sums[slot, 1, 1], jnp.add)
        results[1, slot, 0] = (grad_keys * my_scale(key_scale)).astype(BF16)
        results[1, slot, 1] = grad_values.astype(BF16)
        return_heads(1, slot)

    def queries_arrive(slot):
        wait_rows(QD, slot)
        came_rows(far_stat_copies() if slot == BEYOND else stat_copies(slot))

    def after_outer_scores():
        forward(KV)
        spread(QD, INNER)

    lowest = jnp.full((SLAB, 128), -3e38, F32)
    outer = attend(
        OUTER, (INNER, OUTER), lambda key_slot: wait_rows(KV, key_slot), lowest, after_outer_scores
    )
    settle(OUTER, *outer, 1.0)
    query_side(OUTER, tell(OUTER))
    first = attend(INNER, (INNER, OUTER), lambda key_slot: None, lowest, lambda: None)
    for i in range(3):
        kept[i] = first[i]
    forward(QD)
    row_wide, total, summed = attend(
        INNER, (BEYOND,), lambda key_slot: wait_rows(KV, key_slot), kept[0], lambda: None
    )
    earlier = jnp.exp(kept[0] - row_wide)
    settle(INNER, row_wide, total + kept[1] * earlier, summed + kept[2] * earlier, earlier)
    query_side(INNER, tell(INNER))
    queries_arrive(OUTER)
    key_part(OUTER, OUTER)
    key_part(INNER, OUTER)
    queries_arrive(INNER)
    key_part(OUTER, INNER)
    key_end(OUTER)
    key_part(INNER, INNER)
    queries_arrive(BEYOND)
    key_part(INNER, BEYOND)
    key_end(INNER)

    for kind in range(2):
        pltpu.make_async_copy(landed.at[kind], landed.at[kind], out_recv.at[kind]).wait()
    sent = lists.at[0:2]
    pltpu.make_async_copy(sent, sent, list_send).wait()
    for kind in (KV, QD):
        sent = stage.at[ARRAYS[kind]]
        pltpu.make_async_copy(sent, sent, a2a_send.at[kind]).wait()
        for slot in range(3):
            sent_rows(r_copies(kind, slot))
        y_copy(kind).wait_send()
    for kind in range(2):
        sent = results.at[kind]
        pltpu.make_async_copy(sent, sent, out_send.at[kind]).wait()
    for slot in (OUTER, INNER):
        sent_rows(stat_copies(slot))
    sent_rows(far_stat_copies())


def hand_out(landed, attention, grad_query, grad_key, grad_value, pieces, held, sems):
    targets = (attention, grad_query, grad_key, grad_value)
    loads = [
        pltpu.make_async_copy(landed.at[kind], pieces.at[kind], sems.at[0, kind])
        for kind in range(2)
    ]
    stores = [pltpu.make_async_copy(held.at[i], targets[i], sems.at[1, i]) for i in range(4)]
    for load in loads:
        load.start()
    for i in range(4):
        if i % 2 == 0:
            loads[i // 2].wait()
        for head in range(landed.shape[1]):
            held[i, :, head * HD : (head + 1) * HD] = pieces[i // 2, head, i % 2]
        stores[i].start()
    for store in stores:
        store.wait()


def local(query, key, value, grad_out, query_scale, key_scale, neighbours):
    rows = lax.axis_size("slab") // FT
    columns = lax.axis_size("head") // 2
    chunk, width = query.shape
    out = jax.ShapeDtypeStruct((chunk, width), BF16)
    landing = (2, width // HD, 2, chunk, HD)
    hbm = pl.BlockSpec(memory_space=pltpu.HBM)
    dma = pltpu.SemaphoreType.DMA
    landed = pl.pallas_call(
        functools.partial(kernel, rows, columns),
        out_shape=jax.ShapeDtypeStruct(landing, BF16),
        in_specs=[hbm] * 7,
        out_specs=hbm,
        scratch_shapes=[
            pltpu.VMEM((4, chunk, width), BF16),
            pltpu.VMEM((1, width), F32),
            pltpu.VMEM((1, width), F32),
            pltpu.VMEM(neighbours.shape, jnp.int32),
            pltpu.VMEM((4, 4 * columns, chunk, HD), BF16),
            pltpu.VMEM((4, 3, 3, SLAB, HD), BF16),
            pltpu.VMEM((8, 128), F32),
            pltpu.VMEM((2, 2, 8, 128), F32),
            pltpu.VMEM((2, BLOCKS, 8, SLAB), F32),
            pltpu.VMEM((2, 3, 2, 8, 3 * 128), F32),
            pltpu.VMEM((3, 2, 3 * TILE, 3 * 128), F32),
            pltpu.VMEM((2, 3, 2, 3 * TILE, 3 * 128), BF16),
            pltpu.VMEM((2, 2, SLAB, 128), F32),
            pltpu.VMEM((2, SLAB, 128), F32),
            pltpu.VMEM((3, SLAB, 128), F32),
            pltpu.VMEM((2, 2, 2, 3 * TILE, HD), F32),
            pltpu.VMEM((3, 3, 2, 8, SLAB), F32),
            pltpu.VMEM((2, 3, 3, 8, SLAB), F32),
            pltpu.VMEM((2, 2, 2, SLAB, HD), BF16),
            dma((7,)),
            dma((2,)),
            dma((2, 2)),
            dma,
            dma,
            dma((2, 7)),
            dma((2,)),
            dma((2, 3, 2)),
            dma((2, 2)),
            dma((2, 2)),
            dma((3,)),
            dma((3,)),
            dma((2,)),
            dma((2,)),
        ],
        compiler_params=pltpu.CompilerParams(
            collective_id=0, has_side_effects=True, vmem_limit_bytes=VMEM_BYTES
        ),
        name="tiles",
    )(
        query, key, value, grad_out,
        query_scale.reshape(1, width), key_scale.reshape(1, width), neighbours,
    )
    return pl.pallas_call(
        hand_out,
        out_shape=(out,) * 4,
        in_specs=[hbm],
        out_specs=(hbm,) * 4,
        scratch_shapes=[
            pltpu.VMEM(landing, BF16), pltpu.VMEM((4, chunk, width), BF16), dma((2, 4)),
        ],
        compiler_params=pltpu.CompilerParams(vmem_limit_bytes=VMEM_BYTES),
        name="hand_out",
    )(landed)


def solution(mesh):
    token = P(("slab", "head"), None)
    return jax.shard_map(
        local,
        mesh=mesh,
        in_specs=(token, token, token, token, P(), P(), P("slab", None)),
        out_specs=(token,) * 4,
        check_vma=False,
    )
```

profile of v0, /device:TPU:137, one launch (start us, length us, event | category | flops | bytes accessed | tf_op | source)
XLA Modules:
  0.0 46.3 jit_solution(15754822357311554414)
XLA Ops:
  0.6 43.8 %tiles.1.landed = bf16[2,16,2,32,128]{4,3,2,1,0:T(8,128)(2,1)} custom-call(bf16[32,2048]{1,0:T(8,128)(2,1)} %query.1, bf16[32,2048]{1,0:T(8,128)(2,1)} %key.1, bf16[32,2048]{1,0:T(8,128)(2,1)} %value.1, bf16[32,2048]{1,0:T(8,128)(2,1)} %grad_out.1, f32[1,2048]{1,0:T(1,128)} %bitcast.2, f32[1,2048]{1,0:T(1,128)} %bitcast.3, s32[4,27]{1,0:T(4,128)} %neighbours_in.1), custom_call_target="tpu_custom_call" | custom-call | tf_op jit(solution)/shard_map/tiles/pallas_call | solution.py:511
  44.5 1.8 %hand_out.1 = (bf16[32,2048]{1,0:T(8,128)(2,1)}, bf16[32,2048]{1,0:T(8,128)(2,1)}, bf16[32,2048]{1,0:T(8,128)(2,1)}, bf16[32,2048]{1,0:T(8,128)(2,1)}) custom-call(bf16[2,16,2,32,128]{4,3,2,1,0:T(8,128)(2,1)} %tiles.1.landed), custom_call_target="tpu_custom_call" | custom-call | tf_op jit(solution)/shard_map/hand_out/pallas_call | solution.py:559
where the time goes:
time: 46.5 us; the launch traced here: 46.3 us
  Pallas kernels  45.7 us (98%)
  between operations  0.64 us (1%)
    pallas_call x1, Pallas kernels, local(): pl.pallas_call(functools.partial(kernel, rows, columns), out_shape=jax.Sh...  43.8 us
    pallas_call x1, Pallas kernels, local(): pl.pallas_call(hand_out, out_shape=(out,) * 4, in_specs=[hbm], out_specs=...  1.83 us

commit v1 on v0

--- a/solution.py
+++ b/solution.py
@@ -81,7 +81,7 @@
             (neighbours_in, neighbours),
         ))
     ]
-    for load in (loads[4], *loads[:4], *loads[5:]):
+    for load in (loads[4], *loads[:2]):
         load.start()
 
     slab = lax.axis_index("slab")
@@ -126,6 +126,8 @@
         def _():
             greet([device(y, r_at[side], x), device(y_partner, r_at[side], x)])
 
+    for load in (*loads[2:4], *loads[5:]):
+        load.start()
     listed[...] = jnp.full(listed.shape, -2.0, F32)
 
     def put(which, array):
@@ -169,8 +171,11 @@
         )
 
     def start_rows(copies):
-        for side, copy in copies.items():
-            at_side(side)(copy.start)
+        if 1 in copies:
+            copies[1].start()
+        for side, parity in ((0, 0), (2, 1), (2, 0), (0, 1)):
+            exists = r < rows - 1 if side == 2 else r > 0
+            pl.when(exists & (r % 2 == parity))(copies[side].start)
 
     def sent_rows(copies):
         for side, copy in copies.items():
@@ -277,7 +282,6 @@
     wait_heads(QD, INNER)
     y_copy(QD).start()
     wait_heads(QD, OUTER)
-    spread(QD, OUTER)
 
     def return_heads(kind, slot):
         for to_x in x_at:
@@ -434,6 +438,7 @@
 
     def after_outer_scores():
         forward(KV)
+        spread(QD, OUTER)
         spread(QD, INNER)
 
     lowest = jnp.full((SLAB, 128), -3e38, F32)

time: 46.5 us -> 46.4 us (level)
  the two profiles are of different devices: /device:TPU:137 before, /device:TPU:209 now
where the time goes in v1:
time: 46.4 us; the launch traced here: 46.3 us
  Pallas kernels  45.6 us (98%)
  between operations  0.64 us (1%)
    pallas_call x1, Pallas kernels, local(): pl.pallas_call(functools.partial(kernel, rows, columns), out_shape=jax.Sh...  43.8 us
    pallas_call x1, Pallas kernels, local(): pl.pallas_call(hand_out, out_shape=(out,) * 4, in_specs=[hbm], out_specs=...  1.83 us

profile of v1, /device:TPU:209, one launch (start us, length us, event | category | flops | bytes accessed | tf_op | source)
XLA Modules:
  0.0 46.3 jit_solution(4140749295671740402)
XLA Ops:
  0.6 43.8 %tiles.1.landed = bf16[2,16,2,32,128]{4,3,2,1,0:T(8,128)(2,1)} custom-call(bf16[32,2048]{1,0:T(8,128)(2,1)} %query.1, bf16[32,2048]{1,0:T(8,128)(2,1)} %key.1, bf16[32,2048]{1,0:T(8,128)(2,1)} %value.1, bf16[32,2048]{1,0:T(8,128)(2,1)} %grad_out.1, f32[1,2048]{1,0:T(1,128)} %bitcast.2, f32[1,2048]{1,0:T(1,128)} %bitcast.3, s32[4,27]{1,0:T(4,128)} %neighbours_in.1), custom_call_target="tpu_custom_call" | custom-call | tf_op jit(solution)/shard_map/tiles/pallas_call | solution.py:516
  44.4 1.8 %hand_out.1 = (bf16[32,2048]{1,0:T(8,128)(2,1)}, bf16[32,2048]{1,0:T(8,128)(2,1)}, bf16[32,2048]{1,0:T(8,128)(2,1)}, bf16[32,2048]{1,0:T(8,128)(2,1)}) custom-call(bf16[2,16,2,32,128]{4,3,2,1,0:T(8,128)(2,1)} %tiles.1.landed), custom_call_target="tpu_custom_call" | custom-call | tf_op jit(solution)/shard_map/hand_out/pallas_call | solution.py:564

commit v2 on v1

--- a/solution.py
+++ b/solution.py
@@ -71,7 +71,7 @@
     stage, data, listed, lists, bias, bias_rows, scores, weights, inverses, log_totals, kept, key_sums,
     stats, stats_sent, results,
     in_sem, a2a_send, a2a_recv, list_send, list_recv, halo_send, y_recv, r_recv,
-    stat_send, stat_recv, far_send, far_recv, out_send, out_recv,
+    stat_send, stat_recv, far_send, far_recv, out_send, out_recv, above_sem,
 ):
     loads = [
         pltpu.make_async_copy(source, target, in_sem.at[i])
@@ -121,10 +121,9 @@
 
     greet([device(to_y, r, to_x) for to_y in y_far for to_x in x_at])
     greet([device(y_partner, r, x)])
-    for side in (0, 2):
-        @at_side(side)
-        def _():
-            greet([device(y, r_at[side], x), device(y_partner, r_at[side], x)])
+    @at_side(2)
+    def _():
+        greet([device(y, r_at[2], x), device(y_partner, r_at[2], x)])
 
     for load in (*loads[2:4], *loads[5:]):
         load.start()
@@ -139,8 +138,7 @@
     put(KEY, (raw[0].astype(F32) * key_scale[...]).astype(BF16))
     loads[1].wait()
     put(VALUE, raw[1])
-    row_sides = (r + rows - 1) // rows + (2 * rows - 2 - r) // rows
-    pl.semaphore_wait(barrier, 4 * columns + 1 + 2 * row_sides)
+    pl.semaphore_wait(barrier, 4 * columns + 1 + 2 * ((r + rows - 1) // rows))
 
     my_rows = pl.ds(pl.multiple_of(head * chunk, chunk), chunk)
 
@@ -209,6 +207,14 @@
         came_rows(r_copies(kind, slot))
 
     send_heads(KV, y_far)
+
+    @at_side(0)
+    def _():
+        for to_y in (y, y_partner):
+            pl.semaphore_signal(
+                above_sem, 1, device_id=device(to_y, r_at[0], x), device_id_type=MESH
+            )
+
     loads[6].wait()
     listed[0:TW, 0:27] = neighbours[...].astype(F32)
     for to_y in y_far:
@@ -234,6 +240,11 @@
 
     wait_heads(KV, INNER)
     y_copy(KV).start()
+
+    @at_side(2)
+    def _():
+        pl.semaphore_wait(above_sem, 2)
+
     spread(KV, INNER)
     wait_heads(KV, OUTER)
     spread(KV, OUTER)
@@ -552,6 +563,7 @@
             dma((3,)),
             dma((2,)),
             dma((2,)),
+            pltpu.SemaphoreType.REGULAR,
         ],
         compiler_params=pltpu.CompilerParams(
             collective_id=0, has_side_effects=True, vmem_limit_bytes=VMEM_BYTES

time: 46.4 us -> 46.5 us (level)
  no operation moved by 1% of the time
where the time goes in v2:
time: 46.5 us; the launch traced here: 46.4 us
  Pallas kernels  45.7 us (98%)
  between operations  0.64 us (1%)
    pallas_call x1, Pallas kernels, local(): pl.pallas_call(functools.partial(kernel, rows, columns), out_shape=jax.Sh...  43.9 us
    pallas_call x1, Pallas kernels, local(): pl.pallas_call(hand_out, out_shape=(out,) * 4, in_specs=[hbm], out_specs=...  1.83 us

profile of v2, /device:TPU:209, one launch (start us, length us, event | category | flops | bytes accessed | tf_op | source)
XLA Modules:
  0.0 46.4 jit_solution(8425358386916133902)
XLA Ops:
  0.6 43.9 %tiles.1.landed = bf16[2,16,2,32,128]{4,3,2,1,0:T(8,128)(2,1)} custom-call(bf16[32,2048]{1,0:T(8,128)(2,1)} %query.1, bf16[32,2048]{1,0:T(8,128)(2,1)} %key.1, bf16[32,2048]{1,0:T(8,128)(2,1)} %value.1, bf16[32,2048]{1,0:T(8,128)(2,1)} %grad_out.1, f32[1,2048]{1,0:T(1,128)} %bitcast.2, f32[1,2048]{1,0:T(1,128)} %bitcast.3, s32[4,27]{1,0:T(4,128)} %neighbours_in.1), custom_call_target="tpu_custom_call" | custom-call | tf_op jit(solution)/shard_map/tiles/pallas_call | solution.py:527
  44.5 1.8 %hand_out.1 = (bf16[32,2048]{1,0:T(8,128)(2,1)}, bf16[32,2048]{1,0:T(8,128)(2,1)}, bf16[32,2048]{1,0:T(8,128)(2,1)}, bf16[32,2048]{1,0:T(8,128)(2,1)}) custom-call(bf16[2,16,2,32,128]{4,3,2,1,0:T(8,128)(2,1)} %tiles.1.landed), custom_call_target="tpu_custom_call" | custom-call | tf_op jit(solution)/shard_map/hand_out/pallas_call | solution.py:576

commit v3 on v1

--- a/solution.py
+++ b/solution.py
@@ -406,16 +406,21 @@
         return_heads(0, slot)
 
     def key_part(slot, query_slot):
-        for side in range(2):
+        def half(side, carry):
+            mine = pl.ds(pl.multiple_of(side * 2 * TILE, 2 * TILE), 2 * TILE)
+            seen = pl.ds(pl.multiple_of(side * TILE, TILE), 3 * TILE)
             message = jnp.concatenate(
-                [stats[query_slot, row, slot, :, own(side)] for row in range(3)], axis=1
-            )
-            queries = rows_of(QUERY, query_slot, side)
-            grads = rows_of(GRAD, query_slot, side)
-            part = jnp.exp(add_rows(
-                dot_nt(data[KEY, slot, 1, near(side), :], queries), message[side : side + 3]
-            ))
-            grad_weights = dot_nt(data[VALUE, slot, 1, near(side), :], grads)
+                [stats[query_slot, row, slot, :, mine] for row in range(3)], axis=1
+            )
+            rows_added = jnp.where(side == 0, message[0:3], message[1:4])
+            queries = jnp.concatenate(
+                [data[QUERY, query_slot, row, mine, :] for row in range(3)], axis=0
+            )
+            grads = jnp.concatenate(
+                [data[GRAD, query_slot, row, mine, :] for row in range(3)], axis=0
+            )
+            part = jnp.exp(add_rows(dot_nt(data[KEY, slot, 1, seen, :], queries), rows_added))
+            grad_weights = dot_nt(data[VALUE, slot, 1, seen, :], grads)
             slopes = (part * (grad_weights - message[TW : TW + 1])).astype(BF16)
             for which, term in (
                 (0, dot_nn(slopes, queries)), (1, dot_nn(part.astype(BF16), grads))
@@ -424,6 +429,9 @@
                     key_sums[slot, which, side] = term
                 else:
                     key_sums[slot, which, side] += term
+            return carry
+
+        lax.fori_loop(0, 2, half, 0)
 
     def key_end(slot):
         grad_keys = join(key_sums[slot, 0, 0], key_sums[slot, 0, 1], jnp.add)

time: 46.4 us -> 46.6 us (level)
  no operation moved by 1% of the time
where the time goes in v3:
time: 46.6 us; the launch traced here: 46.4 us
  Pallas kernels  45.8 us (98%)
  between operations  0.64 us (1%)
    pallas_call x1, Pallas kernels, local(): pl.pallas_call(functools.partial(kernel, rows, columns), out_shape=jax.Sh...  44 us
    pallas_call x1, Pallas kernels, local(): pl.pallas_call(hand_out, out_shape=(out,) * 4, in_specs=[hbm], out_specs=...  1.83 us

profile of v3, /device:TPU:209, one launch (start us, length us, event | category | flops | bytes accessed | tf_op | source)
XLA Modules:
  0.0 46.4 jit_solution(8148831455506334563)
XLA Ops:
  0.6 44.0 %tiles.1.landed = bf16[2,16,2,32,128]{4,3,2,1,0:T(8,128)(2,1)} custom-call(bf16[32,2048]{1,0:T(8,128)(2,1)} %query.1, bf16[32,2048]{1,0:T(8,128)(2,1)} %key.1, bf16[32,2048]{1,0:T(8,128)(2,1)} %value.1, bf16[32,2048]{1,0:T(8,128)(2,1)} %grad_out.1, f32[1,2048]{1,0:T(1,128)} %bitcast.2, f32[1,2048]{1,0:T(1,128)} %bitcast.3, s32[4,27]{1,0:T(4,128)} %neighbours_in.1), custom_call_target="tpu_custom_call" | custom-call | tf_op jit(solution)/shard_map/tiles/pallas_call | solution.py:524
  44.6 1.8 %hand_out.1 = (bf16[32,2048]{1,0:T(8,128)(2,1)}, bf16[32,2048]{1,0:T(8,128)(2,1)}, bf16[32,2048]{1,0:T(8,128)(2,1)}, bf16[32,2048]{1,0:T(8,128)(2,1)}) custom-call(bf16[2,16,2,32,128]{4,3,2,1,0:T(8,128)(2,1)} %tiles.1.landed), custom_call_target="tpu_custom_call" | custom-call | tf_op jit(solution)/shard_map/hand_out/pallas_call | solution.py:572
